TPU v7x, 32 devices: a whole 2x2x4 slice. The times are simulated.
32 devices in a mesh: section: 2 (over y), row: 4 (over z), tp: 4 (over x, core).
Axes of the slice: x: 2, y: 2, z: 4, core: 2. Of those that a mesh axis runs over, the one named last changes fastest.
Arguments:
- section_feeds: bfloat16 [2, 2, 128, 8192], P('section', None, None, 'row'), may hold values from -6 to 6
- norm_gain: float32 [2, 8192], P('section', 'row'), may hold values from 0.1 to 1.9
- up_weight: bfloat16 [2, 8192, 32768], P('section', 'row', 'tp'), may hold values from -0.0625 to 0.0625
- down_weight: bfloat16 [2, 32768, 8192], P('section', 'tp', 'row'), may hold values from -0.03125 to 0.03125
Outputs:
- section_ends: bfloat16 [2, 2, 128, 8192], P('section', None, None, 'row')
All inputs are finite; a program needn't handle non-finite values.
Results may differ from a plain program's by a relative error of at most 0.011.
Values may be sent and summed in bfloat16 or wider, within the bound.
A program may use at most 192 MiB of HBM per device.

v0:
```python
import jax
import jax.numpy as jnp
from jax import lax
from jax.sharding import PartitionSpec as P

D = 8192


epsilon = 1e-05
gelu_coeff = 0.7978845608028654


def shifted(array, axis, by):
    devices = lax.axis_size(axis)
    pairs = [(i, i + by) for i in range(devices) if 0 <= i + by < devices]
    return lax.ppermute(array, axis, pairs)


def gelu_value(inputs):
    inner = gelu_coeff * (inputs + 0.044715 * inputs * inputs * inputs)
    return 0.5 * inputs * (1.0 + jnp.tanh(inner))


def gelu_slope(inputs):
    inner = gelu_coeff * (inputs + 0.044715 * inputs * inputs * inputs)
    tangent = jnp.tanh(inner)
    return 0.5 * (1.0 + tangent) + 0.5 * inputs * (1.0 - tangent * tangent) * gelu_coeff * (
        1.0 + 3.0 * 0.044715 * inputs * inputs
    )


def row_pair(first_arr, second_arr):
    return lax.psum((jnp.sum(first_arr, axis=1), jnp.sum(second_arr, axis=1)), "row")


def cross_section(produced, offset_by):
    return shifted(produced, "section", offset_by)


def body(section_feeds, norm_gain, up_weight, down_weight):
    up_local = up_weight[0]
    down_local = down_weight[0]
    gain_row = norm_gain[0]
    feeds_local = section_feeds[0]
    micro_count = feeds_local.shape[0]
    row_count = feeds_local.shape[1]
    width_local = up_local.shape[0]
    hidden_local = up_local.shape[1]
    is_first = lax.axis_index("section") == 0

    def hidden_side(make_term):
        return lax.psum(make_term(0, hidden_local), "row")

    def hidden_contract(activated, fold_step):
        initial = jnp.zeros((row_count, width_local), jnp.float32)
        return fold_step(initial, activated, 0)

    def feature_total(partial_value):
        return lax.psum(partial_value, "tp")

    def pick_saved(early_item, late_item):
        return jnp.where(is_first, early_item, late_item)

    zeros_full = jnp.zeros((row_count, width_local), jnp.bfloat16)
    saved_list = []
    output_parts = []
    received = zeros_full
    for tick_index in range(micro_count + 1):
        feed_rows = feeds_local[min(tick_index, micro_count - 1)]
        arriving = zeros_full if tick_index == 0 else received
        inputs = jnp.where(is_first, feed_rows, arriving)
        values = inputs.astype(jnp.float32)
        row_sum, squares = row_pair(values, values * values)
        row_mean = row_sum / D
        variance = squares / D - row_mean * row_mean
        forward_inv_std = lax.rsqrt(variance + epsilon)
        forward_normed = (values - row_mean[:, None]) * forward_inv_std[:, None]
        scaled = (forward_normed * gain_row[None, :]).astype(jnp.bfloat16)

        def up_term(offset, length):
            return lax.dot_general(
                up_local, scaled, (((0,), (1,)), ((), ())), preferred_element_type=jnp.float32
            )

        forward_hidden_pre = hidden_side(up_term)
        forward_activated = gelu_value(forward_hidden_pre).astype(jnp.bfloat16)

        def forward_fold(running, shard_part, offset):
            return lax.dot_general(
                shard_part, down_local, (((0,), (0,)), ((), ())), preferred_element_type=jnp.float32
            )

        branch = feature_total(hidden_contract(forward_activated, forward_fold))
        produced = (values + branch).astype(jnp.bfloat16)
        produced, saved = (produced, (forward_normed, forward_inv_std, forward_hidden_pre))
        saved_list.append(saved)
        if tick_index >= 1:
            output_parts.append(produced)
        if tick_index < micro_count:
            received = cross_section(produced, 1)
    grad_parts = []
    for tick_index in range(micro_count + 1):
        feed_rows = feeds_local[min(tick_index, micro_count - 1)]
        arriving = zeros_full if tick_index == 0 else received
        incoming = jnp.where(is_first, arriving, feed_rows)
        early_saved = saved_list[max(tick_index - 1, 0)]
        late_saved = saved_list[min(tick_index + 1, micro_count)]
        saved = jax.tree.map(pick_saved, early_saved, late_saved)
        normed, inv_std, hidden_pre = saved

        def back_term(offset, length):
            return lax.dot_general(
                down_local, incoming, (((1,), (1,)), ((), ())), preferred_element_type=jnp.float32
            )

        hidden_grad = hidden_side(back_term)
        pre_grad = (hidden_grad * gelu_slope(hidden_pre)).astype(jnp.bfloat16)

        def backward_fold(running, shard_part, offset):
            return lax.dot_general(
                shard_part, up_local, (((0,), (1,)), ((), ())), preferred_element_type=jnp.float32
            )

        normed_grad = feature_total(hidden_contract(pre_grad, backward_fold)) * gain_row[None, :]
        first_sum, second_sum = row_pair(normed_grad, normed_grad * normed)
        first_mean = first_sum / D
        second_mean = second_sum / D
        result = incoming.astype(jnp.float32) + inv_std[:, None] * (
            normed_grad - first_mean[:, None] - normed * second_mean[:, None]
        )
        produced = result.astype(jnp.bfloat16)
        if tick_index >= 1:
            grad_parts.append(produced)
        if tick_index < micro_count:
            received = cross_section(produced, -1)
    ends_local = jnp.stack(
        [
            jnp.where(is_first, grad_parts[index_value], output_parts[index_value])
            for index_value in range(micro_count)
        ]
    )
    return ends_local[None]


def solution(mesh):
    placed = (
        P("section", None, None, "row"),
        P("section", "row"),
        P("section", "row", "tp"),
        P("section", "tp", "row"),
    )
    return jax.shard_map(
        body, mesh=mesh, in_specs=placed, out_specs=P("section", None, None, "row"), check_vma=False
    )
```

profile of v0, /device:TPU:0, one launch (start us, length us, event | category | flops | bytes accessed | tf_op | source)
XLA Modules:
  0.0 1377.3 jit_solution(10760238137828668280)
XLA Ops:
  6.5 1.2 convert_reduce_fusion.2
  7.8 1.3 fusion.117
  9.0 13.5 all-reduce.6
  22.5 17.3 %fusion.33 = f32[8192,128]{0,1:T(8,128)} fusion(bf16[1,2048,8192]{2,1,0:T(8,128)(2,1)} %param.6, f32[2048]{0:T(1024)} %bitcast.105, f32[128]{0:T(128)S(1)} %get-tuple-element.49, f32[128]{0:T(128)S(1)} %get-tuple-element.48, pred[]{:T(512)S(6)} %eq.3, bf16[1,2,128,2048]{3,2,1,0:T(8,128)(2,1)} %param.4), kind=kOutput, calls=%fused_computation.27 | convolution fusion | flops 4296540160 | bytes 38282240 | tf_op jit(solution)/shard_map/dot_general | solution.py:81
  39.8 0.0 all-reduce.18.cloned.1.call-update
  39.8 0.0 copy-start
  39.8 0.0 all-reduce.20.cloned.1.call-start
  39.9 153.3 %all-reduce.18.cloned.1.call-done = f32[8192,128]{0,1:T(8,128)} async-done(((f32[8192,128]{0,1:T(8,128)}), f32[8192,128]{0,1:T(8,128)}) %all-reduce.18.cloned.1.call-update) | async-done | bytes 4194320 | tf_op jit(solution)/shard_map/psum | solution.py:52
  193.2 17.9 %fusion.10 = f32[128,2048]{1,0:T(8,128)} fusion(bf16[1,8192,2048]{2,1,0:T(8,128)(2,1)} %param.7, f32[8192,128]{0,1:T(8,128)} %all-reduce.18.cloned.1.call-done), kind=kOutput, calls=%fused_computation.10 | convolution fusion | flops 4304404480 | bytes 38797312 | tf_op jit(solution)/shard_map/dot_general | solution.py:89
  211.0 0.0 all-reduce.20.cloned.1.call-update
  211.1 0.0 all-reduce.32.cloned.1.call-start
  211.1 35.2 %all-reduce.20.cloned.1.call-done = f32[128,2048]{1,0:T(8,128)} async-done(((f32[128,2048]{1,0:T(8,128)}), f32[128,2048]{1,0:T(8,128)}) %all-reduce.20.cloned.1.call-update) | async-done | bytes 1048592 | tf_op jit(solution)/shard_map/psum | solution.py:59
  246.3 1.4 fusion.118
  247.7 0.0 copy-start.5
  247.7 3.9 collective-permute-start
  251.6 17.4 %fusion.24 = f32[8192,128]{0,1:T(8,128)} fusion(bf16[1,8192,2048]{2,1,0:T(8,128)(2,1)} %param.7, pred[]{:T(512)S(6)} %eq.3, bf16[1,2,128,2048]{3,2,1,0:T(8,128)(2,1)S(1)} %copy-done), kind=kOutput, calls=%fused_computation.24 | convolution fusion | flops 4295229440 | bytes 38273024 | tf_op jit(solution)/shard_map/dot_general | solution.py:112
  268.9 0.0 collective-permute-done
  268.9 0.3 convert_reduce_fusion.1
  269.3 11.7 all-reduce.5
  281.0 17.1 %fusion.36 = f32[8192,128]{0,1:T(8,128)} fusion(bf16[1,2048,8192]{2,1,0:T(8,128)(2,1)} %param.6, bf16[128,2048]{1,0:T(8,128)(2,1)S(1)} %get-tuple-element.42, f32[2048]{0:T(1024)S(1)} %bitcast.106, f32[128]{0:T(128)S(1)} %get-tuple-element.40, f32[128]{0:T(128)S(1)} %get-tuple-element.47), kind=kOutput, calls=%fused_computation.28 | convolution fusion | flops 4296278016 | bytes 38282240 | tf_op jit(solution)/shard_map/dot_general | solution.py:81
  298.1 0.0 all-reduce.32.cloned.1.call-update
  298.1 0.2 all-reduce.28.cloned.1.call-start
  298.4 288.2 %all-reduce.32.cloned.1.call-done = (f32[8192,128]{0,1:T(8,128)}, f32[8192,128]{0,1:T(8,128)}) async-done(((f32[8192,128]{0,1:T(8,128)}, f32[8192,128]{0,1:T(8,128)}), (f32[8192,128]{0,1:T(8,128)}, f32[8192,128]{0,1:T(8,128)})) %all-reduce.32.cloned.1.call-update) | async-done | bytes 8388624 | tf_op jit(solution)/shard_map/psum | solution.py:52
  586.5 17.8 %fusion.6 = f32[128,2048]{1,0:T(8,128)} fusion(bf16[1,8192,2048]{2,1,0:T(8,128)(2,1)} %param.7, f32[8192,128]{0,1:T(8,128)} %get-tuple-element.33), kind=kOutput, calls=%fused_computation.6 | convolution fusion | flops 4304404480 | bytes 38797312 | tf_op jit(solution)/shard_map/dot_general | solution.py:89
  604.4 18.6 %fusion.18 = f32[128,2048]{1,0:T(8,128)} fusion(bf16[1,2048,8192]{2,1,0:T(8,128)(2,1)} %param.6, f32[8192,128]{0,1:T(8,128)} %get-tuple-element.34, f32[8192,128]{0,1:T(8,128)} %all-reduce.18.cloned.1.call-done, f32[8192,128]{0,1:T(8,128)} %get-tuple-element.33, pred[]{:T(512)S(6)} %eq.3), kind=kOutput, calls=%fused_computation.18 | convolution fusion | flops 4315938816 | bytes 47185920 | tf_op jit(solution)/shard_map/dot_general | solution.py:120
  623.0 0.0 all-reduce.28.cloned.1.call-update
  623.0 0.0 all-reduce.30.cloned.1.call-start
  623.1 50.7 %all-reduce.28.cloned.1.call-done = (f32[128,2048]{1,0:T(8,128)}, f32[128,2048]{1,0:T(8,128)}) async-done(((f32[128,2048]{1,0:T(8,128)}, f32[128,2048]{1,0:T(8,128)}), (f32[128,2048]{1,0:T(8,128)}, f32[128,2048]{1,0:T(8,128)})) %all-reduce.28.cloned.1.call-update) | async-done | bytes 2097168 | tf_op jit(solution)/shard_map/psum | solution.py:59
  673.8 1.4 fusion.130
  675.2 3.4 collective-permute-start.2
  678.6 11.1 collective-permute-done.2
  689.7 0.0 copy-done.2
  689.7 2.0 multiply_reduce_fusion.5
  691.7 11.7 all-reduce.4
  703.4 0.8 add_convert_fusion.2
  704.2 1.5 collective-permute-start.1
  705.8 17.1 %fusion.39 = f32[8192,128]{0,1:T(8,128)} fusion(bf16[1,2048,8192]{2,1,0:T(8,128)(2,1)} %param.6, bf16[128,2048]{1,0:T(8,128)(2,1)S(1)} %get-tuple-element.45, f32[128]{0:T(128)S(1)} %get-tuple-element.38, f32[128]{0:T(128)S(1)} %get-tuple-element.46, f32[2048]{0:T(1024)S(1)} %bitcast.109), kind=kOutput, calls=%fused_computation.29 | convolution fusion | flops 4296278016 | bytes 38282240 | tf_op jit(solution)/shard_map/dot_general | solution.py:81
  722.9 0.0 collective-permute-done.1
  722.9 17.4 %fusion.27 = f32[8192,128]{0,1:T(8,128)} fusion(bf16[1,8192,2048]{2,1,0:T(8,128)(2,1)} %param.7, bf16[128,2048]{1,0:T(8,128)(2,1)S(1)} %collective-permute-done.1, pred[]{:T(512)S(6)} %eq.3, bf16[1,2,128,2048]{3,2,1,0:T(8,128)(2,1)S(1)} %copy-done), kind=kOutput, calls=%fused_computation.25 | convolution fusion | flops 4295229440 | bytes 38797312 | tf_op jit(solution)/shard_map/dot_general | solution.py:112
  740.3 0.0 all-reduce.30.cloned.1.call-update
  740.3 0.0 all-reduce.22.cloned.1.call-start
  740.3 290.3 %all-reduce.30.cloned.1.call-done = (f32[8192,128]{0,1:T(8,128)}, f32[8192,128]{0,1:T(8,128)}) async-done(((f32[8192,128]{0,1:T(8,128)}, f32[8192,128]{0,1:T(8,128)}), (f32[8192,128]{0,1:T(8,128)}, f32[8192,128]{0,1:T(8,128)})) %all-reduce.30.cloned.1.call-update) | async-done | bytes 8388624 | tf_op jit(solution)/shard_map/psum | solution.py:52
  1030.6 18.6 %fusion.14 = f32[128,2048]{1,0:T(8,128)} fusion(bf16[1,2048,8192]{2,1,0:T(8,128)(2,1)} %param.6, f32[8192,128]{0,1:T(8,128)} %get-tuple-element.32, f32[8192,128]{0,1:T(8,128)} %all-reduce.18.cloned.1.call-done, f32[8192,128]{0,1:T(8,128)} %get-tuple-element.31, pred[]{:T(512)S(6)} %eq.3), kind=kOutput, calls=%fused_computation.14 | convolution fusion | flops 4315938816 | bytes 47185920 | tf_op jit(solution)/shard_map/dot_general | solution.py:120
  1049.2 0.0 all-reduce.22.cloned.1.call-update
  1049.2 0.0 all-reduce.24.cloned.1.call-start
  1049.3 35.2 %all-reduce.22.cloned.1.call-done = f32[128,2048]{1,0:T(8,128)} async-done(((f32[128,2048]{1,0:T(8,128)}), f32[128,2048]{1,0:T(8,128)}) %all-reduce.22.cloned.1.call-update) | async-done | bytes 1048592 | tf_op jit(solution)/shard_map/psum | solution.py:59
  1084.5 1.7 multiply_reduce_fusion.4
  1086.3 11.7 all-reduce.3
  1098.0 3.0 select_bitcast_fusion
  1101.0 1.3 collective-permute-start.3
  1102.3 11.8 collective-permute-done.3
  1114.0 17.4 %fusion.30 = f32[8192,128]{0,1:T(8,128)} fusion(bf16[1,8192,2048]{2,1,0:T(8,128)(2,1)} %param.7, bf16[128,2048]{1,0:T(8,128)(2,1)S(1)} %collective-permute-done.3, pred[]{:T(512)S(6)} %eq.3, bf16[1,2,128,2048]{3,2,1,0:T(8,128)(2,1)S(1)} %copy-done), kind=kOutput, calls=%fused_computation.26 | convolution fusion | flops 4295229440 | bytes 38797312 | tf_op jit(solution)/shard_map/dot_general | solution.py:112
  1131.4 0.0 all-reduce.24.cloned.1.call-update
  1131.4 0.3 all-reduce.26.cloned.1.call-start
  1131.7 18.6 %fusion = f32[128,2048]{1,0:T(8,128)} fusion(bf16[1,8192,2048]{2,1,0:T(8,128)(2,1)} %param.7, f32[8192,128]{0,1:T(8,128)} %get-tuple-element.31), kind=kOutput, calls=%fused_computation | convolution fusion | flops 4304404480 | bytes 38797312 | tf_op jit(solution)/shard_map/dot_general | solution.py:89
  1150.4 133.2 %all-reduce.24.cloned.1.call-done = f32[8192,128]{0,1:T(8,128)} async-done(((f32[8192,128]{0,1:T(8,128)}), f32[8192,128]{0,1:T(8,128)}) %all-reduce.24.cloned.1.call-update) | async-done | bytes 4194320 | tf_op jit(solution)/shard_map/psum | solution.py:52
  1283.6 18.6 %fusion.12 = f32[128,2048]{1,0:T(8,128)} fusion(bf16[1,2048,8192]{2,1,0:T(8,128)(2,1)} %param.6, f32[8192,128]{0,1:T(8,128)} %all-reduce.24.cloned.1.call-done, f32[8192,128]{0,1:T(8,128)} %get-tuple-element.33, f32[8192,128]{0,1:T(8,128)} %get-tuple-element.31, pred[]{:T(512)S(6)} %eq.3), kind=kOutput, calls=%fused_computation.12 | convolution fusion | flops 4315938816 | bytes 47185920 | tf_op jit(solution)/shard_map/dot_general | solution.py:120
  1302.2 0.0 all-reduce.26.cloned.1.call-update
  1302.3 50.7 %all-reduce.26.cloned.1.call-done = (f32[128,2048]{1,0:T(8,128)}, f32[128,2048]{1,0:T(8,128)}) async-done(((f32[128,2048]{1,0:T(8,128)}, f32[128,2048]{1,0:T(8,128)}), (f32[128,2048]{1,0:T(8,128)}, f32[128,2048]{1,0:T(8,128)})) %all-reduce.26.cloned.1.call-update) | async-done | bytes 2097168 | tf_op jit(solution)/shard_map/psum | solution.py:59
  1353.0 1.7 multiply_reduce_fusion.3
  1354.7 11.7 all-reduce.2
  1366.5 2.5 fusion.151
  1369.0 0.0 copy-done.4
  1369.0 1.1 maximum_bitcast_fusion
  (18 shorter events, 0.1 us)
Async XLA Ops:
  6.5 186.6 %all-reduce.18.cloned.1.call-start = ((), (), s32[]{:S(2)}) async-start(), calls=%async_computation | async-start | bytes 8388608 | tf_op jit(solution)/shard_map/psum | solution.py:52
  39.8 206.5 %copy-start = (bf16[1,2,128,2048]{3,2,1,0:T(8,128)(2,1)S(1)}, bf16[1,2,128,2048]{3,2,1,0:T(8,128)(2,1)}, u32[]{:S(2)}) copy-start(bf16[1,2,128,2048]{3,2,1,0:T(8,128)(2,1)} %param.4) | copy-start | bytes 3145732
  39.8 206.5 %all-reduce.20.cloned.1.call-start = ((), (), s32[]{:S(2)}) async-start(), calls=%async_computation.1 | async-start | bytes 2097152 | tf_op jit(solution)/shard_map/psum | solution.py:59
  211.1 375.5 %all-reduce.32.cloned.1.call-start = ((), (), s32[]{:S(2)}) async-start(), calls=%async_computation.7 | async-start | bytes 16777216 | tf_op jit(solution)/shard_map/psum | solution.py:52
  247.7 33.3 %copy-start.5 = (f32[1,2048]{1,0:T(1,128)S(1)}, f32[1,2048]{1,0:T(1,128)}, u32[]{:S(2)}) copy-start(f32[1,2048]{1,0:T(1,128)} %param.5) | copy-start | bytes 24580
  247.7 21.2 %collective-permute-start = (bf16[128,2048]{1,0:T(8,128)(2,1)S(1)}, bf16[128,2048]{1,0:T(8,128)(2,1)S(1)}, u32[]{:S(2)}, u32[]{:S(2)}) collective-permute-start(bf16[128,2048]{1,0:T(8,128)(2,1)S(1)} %fusion.118), channel_id=1, source_target_pairs={{0,16},{1,17},{2,18},{3,19},{4,20},{5,21},{6,22},{7,23},{8,24},{9,... | collective-permute-start | bytes 1572872 | tf_op jit(solution)/shard_map/ppermute | solution.py:16
  298.1 375.6 %all-reduce.28.cloned.1.call-start = ((), (), s32[]{:S(2)}) async-start(), calls=%async_computation.5 | async-start | bytes 4194304 | tf_op jit(solution)/shard_map/psum | solution.py:59
  623.0 407.6 %all-reduce.30.cloned.1.call-start = ((), (), s32[]{:S(2)}) async-start(), calls=%async_computation.6 | async-start | bytes 16777216 | tf_op jit(solution)/shard_map/psum | solution.py:52
  673.8 29.6 %copy-start.1 = (f32[128,2048]{1,0:T(8,128)S(1)}, f32[128,2048]{1,0:T(8,128)}, u32[]{:S(2)}) copy-start(f32[128,2048]{1,0:T(8,128)} %get-tuple-element.18) | copy-start | bytes 3145732
  675.2 14.5 %copy-start.2 = (bf16[128,2048]{1,0:T(8,128)(2,1)}, bf16[128,2048]{1,0:T(8,128)(2,1)S(1)}, u32[]{:S(2)}) copy-start(bf16[128,2048]{1,0:T(8,128)(2,1)S(1)} %fusion.130) | copy-start | bytes 1572868
  675.2 14.5 %collective-permute-start.2 = (bf16[128,2048]{1,0:T(8,128)(2,1)S(1)}, bf16[128,2048]{1,0:T(8,128)(2,1)S(1)}, u32[]{:S(2)}, u32[]{:S(2)}) collective-permute-start(bf16[128,2048]{1,0:T(8,128)(2,1)S(1)} %fusion.130), channel_id=1, source_target_pairs={{0,16},{1,17},{2,18},{3,19},{4,20},{5,21},{6,22},{7,23},{8,24},{9,... | collective-permute-start | bytes 1572872 | tf_op jit(solution)/shard_map/ppermute | solution.py:16
  704.2 18.6 %collective-permute-start.1 = (bf16[128,2048]{1,0:T(8,128)(2,1)S(1)}, bf16[128,2048]{1,0:T(8,128)(2,1)S(1)}, u32[]{:S(2)}, u32[]{:S(2)}) collective-permute-start(bf16[128,2048]{1,0:T(8,128)(2,1)S(1)} %add_convert_fusion.2), channel_id=1, source_target_pairs={{16,0},{17,1},{18,2},{19,3},{20,4},{21,5},{22,6},{23,7},{24,8},{25... | collective-permute-start | bytes 1572872 | tf_op jit(solution)/shard_map/ppermute | solution.py:16
  740.3 344.2 %all-reduce.22.cloned.1.call-start = ((), (), s32[]{:S(2)}) async-start(), calls=%async_computation.2 | async-start | bytes 2097152 | tf_op jit(solution)/shard_map/psum | solution.py:59
  1030.6 67.4 %copy-start.3 = (bf16[128,2048]{1,0:T(8,128)(2,1)S(1)}, bf16[128,2048]{1,0:T(8,128)(2,1)}, u32[]{:S(2)}) copy-start(bf16[128,2048]{1,0:T(8,128)(2,1)} %copy-done.2) | copy-start | bytes 1572868
  1049.2 234.4 %all-reduce.24.cloned.1.call-start = ((), (), s32[]{:S(2)}) async-start(), calls=%async_computation.3 | async-start | bytes 8388608 | tf_op jit(solution)/shard_map/psum | solution.py:52
  1101.0 13.1 collective-permute-start.3
  1131.4 221.6 %all-reduce.26.cloned.1.call-start = ((), (), s32[]{:S(2)}) async-start(), calls=%async_computation.4 | async-start | bytes 4194304 | tf_op jit(solution)/shard_map/psum | solution.py:59
  1302.2 66.7 %copy-start.4 = (bf16[1,128,2048]{2,1,0:T(8,128)(2,1)S(1)}, bf16[1,128,2048]{2,1,0:T(8,128)(2,1)}, u32[]{:S(2)}) copy-start(bf16[1,128,2048]{2,1,0:T(8,128)(2,1)} %get-tuple-element.35) | copy-start | bytes 1572868
Sparse Core Ops, SparseCore 0:
  39.9 153.1 all-reduce.17
  211.2 35.1 all-reduce.19
  298.2 288.2 all-reduce.31
  623.2 50.5 all-reduce.27
  740.4 290.1 all-reduce.29
  1049.3 35.1 all-reduce.21
  1131.5 152.0 all-reduce.23
  1302.4 50.5 all-reduce.25
where the time goes:
time: 1390 us; the launch traced here: 1380 us
  waiting for transfers between devices  1060 us (76%)
  matrix products  214 us (15%)
  blocking collectives  60.3 us (4%)
  other arithmetic  18.5 us (1%)
  between operations  14.1 us (1%)
    psum x4, waiting for transfers between devices, hidden_side(): return lax.psum(make_term(0, hidden_local), 'row')  865 us
    psum x4, waiting for transfers between devices, feature_total(): return lax.psum(partial_value, 'tp')  172 us
    psum x5, blocking collectives, row_pair(): lax.psum((jnp.sum(first_arr, axis=1), jnp.sum(second_arr, axis=1)), 'row')  60.3 us
    dot_general x3, matrix products, backward_fold(): lax.dot_general(shard_part, up_local, (((0,), (1,)), ((), ())), preferred...  55.8 us
    dot_general x3, matrix products, forward_fold(): lax.dot_general(shard_part, down_local, (((0,), (0,)), ((), ())), preferr...  54.4 us
    dot_general x3, matrix products, back_term(): lax.dot_general(down_local, incoming, (((1,), (1,)), ((), ())), preferred...  52.1 us
    dot_general x3, matrix products, up_term(): lax.dot_general(up_local, scaled, (((0,), (1,)), ((), ())), preferred_ele...  51.6 us
  transfers between devices with their start and end apart: 12, of which 10 were waited for; matrix products, arithmetic and copies ran while one was open for 4% of the time, Pallas kernels for 0%

commit v1 on v0

v1 whole, which is shorter than its diff:
```python
import jax
import jax.numpy as jnp
from jax import lax
from jax.sharding import PartitionSpec as P

D = 8192


epsilon = 1e-05
gelu_coeff = 0.7978845608028654


def shifted(array, axis, by):
    devices = lax.axis_size(axis)
    pairs = [(i, i + by) for i in range(devices) if 0 <= i + by < devices]
    return lax.ppermute(array, axis, pairs)


def gelu_value(inputs):
    inner = gelu_coeff * (inputs + 0.044715 * inputs * inputs * inputs)
    return 0.5 * inputs * (1.0 + jnp.tanh(inner))


def gelu_slope(inputs):
    inner = gelu_coeff * (inputs + 0.044715 * inputs * inputs * inputs)
    tangent = jnp.tanh(inner)
    return 0.5 * (1.0 + tangent) + 0.5 * inputs * (1.0 - tangent * tangent) * gelu_coeff * (
        1.0 + 3.0 * 0.044715 * inputs * inputs
    )


def row_pair(first_arr, second_arr):
    return lax.psum((jnp.sum(first_arr, axis=1), jnp.sum(second_arr, axis=1)), "row")


def body(section_feeds, norm_gain, up_weight, down_weight):
    up_local = up_weight[0]
    down_local = down_weight[0]
    gain_row = norm_gain[0]
    feeds_local = section_feeds[0]
    micro_count = feeds_local.shape[0]
    is_first = lax.axis_index("section") == 0

    def hidden_total(term):
        return lax.psum(term.astype(jnp.bfloat16), "row").astype(jnp.float32)

    def feature_total(term):
        return lax.psum(term.astype(jnp.bfloat16), "tp").astype(jnp.float32)

    def up_term(scaled):
        return lax.dot_general(
            up_local, scaled, (((0,), (1,)), ((), ())), preferred_element_type=jnp.float32
        )

    def back_term(incoming):
        return lax.dot_general(
            down_local, incoming, (((1,), (1,)), ((), ())), preferred_element_type=jnp.float32
        )

    def forward_fold(activated):
        return lax.dot_general(
            activated, down_local, (((0,), (0,)), ((), ())), preferred_element_type=jnp.float32
        )

    def backward_fold(pre_grad):
        return lax.dot_general(
            pre_grad, up_local, (((0,), (1,)), ((), ())), preferred_element_type=jnp.float32
        )

    def normalise(inputs):
        values = inputs.astype(jnp.float32)
        row_sum, squares = row_pair(values, values * values)
        row_mean = row_sum / D
        variance = squares / D - row_mean * row_mean
        inv_std = lax.rsqrt(variance + epsilon)
        normed = (values - row_mean[:, None]) * inv_std[:, None]
        return (normed * gain_row[None, :]).astype(jnp.bfloat16), normed, inv_std

    def activate(hidden_pre):
        return gelu_value(hidden_pre).astype(jnp.bfloat16)

    def slope_times(hidden_grad, hidden_pre):
        return (hidden_grad * gelu_slope(hidden_pre)).astype(jnp.bfloat16)

    def residual(inputs, branch):
        return (inputs.astype(jnp.float32) + branch).astype(jnp.bfloat16)

    def input_grad(incoming, folded, normed, inv_std):
        normed_grad = folded * gain_row[None, :]
        first_sum, second_sum = row_pair(normed_grad, normed_grad * normed)
        result = incoming.astype(jnp.float32) + inv_std[:, None] * (
            normed_grad - (first_sum / D)[:, None] - normed * (second_sum / D)[:, None]
        )
        return result.astype(jnp.bfloat16)

    feeds = [feeds_local[index] for index in range(micro_count)]
    last = micro_count - 1
    outputs = [None] * micro_count
    grads = [None] * micro_count
    saved = [None] * micro_count
    early_grad = None
    middle = None
    back = None

    scaled, normed, inv_std = normalise(feeds[0])
    total = hidden_total(
        lax.cond(is_first, lambda: up_term(scaled), lambda: back_term(feeds[0]))
    )
    early_grad = total
    first_saved = [(normed, inv_std, total)]
    middle = residual(feeds[0], feature_total(forward_fold(activate(total))))
    middle = shifted(middle, "section", 1)

    for index in range(micro_count):
        if index < last:
            inputs = jnp.where(is_first, feeds[index + 1], middle)
            scaled, normed, inv_std = normalise(inputs)
            total = hidden_total(up_term(scaled))
            first_saved.append((normed, inv_std, total))
            late_saved = (normed, inv_std, total)
            produced = residual(inputs, feature_total(forward_fold(activate(total))))
            outputs[index] = produced
            middle = shifted(produced, "section", 1)
        else:
            scaled, normed, inv_std = normalise(middle)
            late_saved = (normed, inv_std, None)
            incoming = back
            total = hidden_total(
                lax.cond(is_first, lambda: back_term(incoming), lambda: up_term(scaled))
            )
            late_saved = (normed, inv_std, total)
            prior_normed, prior_inv, prior_pre = first_saved[index - 1]
            folded = feature_total(
                lax.cond(
                    is_first,
                    lambda: backward_fold(slope_times(total, prior_pre)),
                    lambda: forward_fold(activate(total)),
                )
            )
            outputs[index] = residual(middle, folded)
            grads[index - 1] = input_grad(incoming, folded, prior_normed, prior_inv)
            early_grad = hidden_total(back_term(feeds[index]))
        normed, inv_std, hidden_pre = late_saved
        folded = feature_total(backward_fold(slope_times(early_grad, hidden_pre)))
        back = shifted(input_grad(feeds[index], folded, normed, inv_std), "section", -1)

    normed, inv_std, hidden_pre = first_saved[last]
    total = hidden_total(back_term(back))
    folded = feature_total(backward_fold(slope_times(total, hidden_pre)))
    grads[last] = input_grad(back, folded, normed, inv_std)
    ends_local = jnp.stack(
        [jnp.where(is_first, grads[index], outputs[index]) for index in range(micro_count)]
    )
    return ends_local[None]


def solution(mesh):
    placed = (
        P("section", None, None, "row"),
        P("section", "row"),
        P("section", "row", "tp"),
        P("section", "tp", "row"),
    )
    return jax.shard_map(
        body, mesh=mesh, in_specs=placed, out_specs=P("section", None, None, "row"), check_vma=False
    )
```

time: 1390 us -> 903 us (0.65)
  waiting for transfers between devices: 1060 us -> 570 us
  local copies, waits for them, and re-layouts: 0.03 us -> 20.9 us
  matrix products: 214 us -> 194 us
    psum x8, waiting for transfers between devices: 1040 us -> 537 us  [the longest x4 403 us: hidden_total(): return lax.psum(term.astype(jnp.bfloat16), 'row').astype(jnp.float32)]
    dot_general x3 -> x2, matrix products: 51.6 us -> 31.9 us  [up_term(): lax.dot_general(up_local, scaled, (((0,), (1,)), ((), ())), preferred_ele...]
  transfers between devices with their start and end apart: 12 -> 12, of which waited for: 10 -> 11; matrix products, arithmetic and copies ran while one was open for 4% -> 3% of each run, Pallas kernels for 0% -> 0%
where the time goes in v1:
time: 903 us; the launch traced here: 895 us
  waiting for transfers between devices  570 us (63%)
  matrix products  194 us (21%)
  blocking collectives  60.2 us (7%)
  other arithmetic  24.2 us (3%)
  local copies, waits for them, and re-layouts  20.9 us (2%)
  between operations  14.1 us (2%)
  starting transfers between devices  10.9 us (1%)
    psum x4, waiting for transfers between devices, hidden_total(): return lax.psum(term.astype(jnp.bfloat16), 'row').astype(jnp.float32)  403 us
    psum x4, waiting for transfers between devices, feature_total(): return lax.psum(term.astype(jnp.bfloat16), 'tp').astype(jnp.float32)  134 us
    dot_general x4, matrix products, backward_fold(): lax.dot_general(pre_grad, up_local, (((0,), (1,)), ((), ())), preferred_e...  71.3 us
    psum x5, blocking collectives, row_pair(): lax.psum((jnp.sum(first_arr, axis=1), jnp.sum(second_arr, axis=1)), 'row')  60.2 us
    dot_general x3, matrix products, back_term(): lax.dot_general(down_local, incoming, (((1,), (1,)), ((), ())), preferred...  56.6 us
    dot_general x2, matrix products, forward_fold(): lax.dot_general(activated, down_local, (((0,), (0,)), ((), ())), preferre...  34.3 us
    ppermute x4, waiting for transfers between devices, shifted(): return lax.ppermute(array, axis, pairs)  32.9 us
    dot_general x2, matrix products, up_term(): lax.dot_general(up_local, scaled, (((0,), (1,)), ((), ())), preferred_ele...  31.9 us
  transfers between devices with their start and end apart: 12, of which 11 were waited for; matrix products, arithmetic and copies ran while one was open for 3% of the time, Pallas kernels for 0%

profile of v1, /device:TPU:0, one launch (start us, length us, event | category | flops | bytes accessed | tf_op | source)
XLA Modules:
  0.0 894.6 jit_solution(17841670717596160711)
XLA Ops:
  6.5 1.3 convert_reduce_fusion
  7.8 1.1 slice_bitcast_fusion
  8.9 13.5 %all-reduce.4 = (f32[128]{0:T(128)S(1)}, f32[128]{0:T(128)S(1)}) all-reduce(f32[128]{0:T(128)S(1)} %get-tuple-element.59, f32[128]{0:T(128)S(1)} %get-tuple-element.58), channel_id=1, replica_groups=mesh['section'=2,'row'=4,'tp'=4] {'row'}, use_global_device_ids=true, to_apply=%region_3.0 | all-reduce | flops 256 | bytes 2048 | tf_op jit(solution)/shard_map/psum | solution.py:33
  22.4 1.4 fusion.117
  23.8 15.3 %conditional.3 = (bf16[8192,128]{1,0:T(8,128)(2,1)S(1)}) conditional(s32[]{:T(128)} %convert_element_type.151, (bf16[8192,2048]{1,0:T(8,128)(2,1)}, bf16[128,2048]{1,0:T(8,128)(2,1)S(1)}) %tuple.73, (bf16[2048,8192]{1,0:T(8,128)(2,1)}, bf16[128,2048]{1,0:T(8,128)(2,1)S(1)}) %tuple.76), branch_computations={%region_4.0_spmd, %region_5.0_spmd} | conditional | flops 4294967296 | bytes 36175880 | solution.py:107
  23.8 15.3 %fusion.168 = bf16[8192,128]{1,0:T(8,128)(2,1)S(1)} fusion(bf16[2048,8192]{1,0:T(8,128)(2,1)} %get-tuple-element.42, bf16[128,2048]{1,0:T(8,128)(2,1)S(1)} %get-tuple-element.43), kind=kOutput, calls=%fused_computation.222 | convolution fusion | flops 4294967296 | bytes 36175872 | tf_op jit(solution)/shard_map/cond/branch_1_fun/dot_general | solution.py:51
  39.2 3.0 copy.5
  42.1 0.0 all-reduce.17.cloned.1.call-update
  42.2 0.2 all-reduce.19.cloned.1.call-start
  42.4 84.6 %all-reduce.17.cloned.1.call-done = bf16[8192,128]{0,1:T(8,128)(2,1)} async-done(((bf16[8192,128]{0,1:T(8,128)(2,1)}), bf16[8192,128]{0,1:T(8,128)(2,1)}) %all-reduce.17.cloned.1.call-update) | async-done | bytes 2097168 | tf_op jit(solution)/shard_map/psum | solution.py:45
  127.0 17.1 %convolution_convert_fusion.7 = bf16[128,2048]{1,0:T(8,128)(2,1)} fusion(bf16[8192,128]{0,1:T(8,128)(2,1)} %all-reduce.17.cloned.1.call-done, bf16[1,8192,2048]{2,1,0:T(8,128)(2,1)} %param.13), kind=kOutput, calls=%fused_computation.84 | convolution fusion | flops 4305715200 | bytes 36175872 | tf_op jit(solution)/shard_map/dot_general | solution.py:61
  144.1 0.0 all-reduce.19.cloned.1.call-update
  144.2 0.0 all-reduce.21.cloned.1.call-start
  144.2 32.2 %all-reduce.19.cloned.1.call-done = bf16[128,2048]{1,0:T(8,128)(2,1)} async-done(((bf16[128,2048]{1,0:T(8,128)(2,1)}), bf16[128,2048]{1,0:T(8,128)(2,1)}) %all-reduce.19.cloned.1.call-update) | async-done | bytes 524304 | tf_op jit(solution)/shard_map/psum | solution.py:48
  176.5 1.2 fusion.119
  177.6 3.4 collective-permute-start
  181.1 10.2 %collective-permute-done = bf16[128,2048]{1,0:T(8,128)(2,1)S(1)} collective-permute-done((bf16[128,2048]{1,0:T(8,128)(2,1)S(1)}, bf16[128,2048]{1,0:T(8,128)(2,1)S(1)}, u32[]{:S(2)}, u32[]{:S(2)}) %collective-permute-start) | collective-permute-done | bytes 524320 | tf_op jit(solution)/shard_map/ppermute | solution.py:16
  191.3 0.3 fusion.85
  191.6 11.7 %all-reduce.3 = (f32[128]{0:T(128)S(1)}, f32[128]{0:T(128)S(1)}) all-reduce(f32[128]{0:T(128)S(1)} %get-tuple-element.71, f32[128]{0:T(128)S(1)} %get-tuple-element.70), channel_id=1, replica_groups=mesh['section'=2,'row'=4,'tp'=4] {'row'}, use_global_device_ids=true, to_apply=%region_11.12 | all-reduce | flops 256 | bytes 2048 | tf_op jit(solution)/shard_map/psum | solution.py:33
  203.3 16.5 %fusion.35 = bf16[8192,128]{0,1:T(8,128)(2,1)} fusion(bf16[128,2048]{1,0:T(8,128)(2,1)S(1)} %get-tuple-element.94, f32[128]{0:T(128)S(1)} %get-tuple-element.103, f32[128]{0:T(128)S(1)} %get-tuple-element.102, f32[2048]{0:T(1024)S(1)} %bitcast.69, bf16[1,2048,8192]{2,1,0:T(8,128)(2,1)} %param.12), kind=kOutput, calls=%fused_computation.46 | convolution fusion | flops 4297326592 | bytes 36185088 | tf_op jit(solution)/shard_map/dot_general | solution.py:51
  219.8 0.3 all-reduce.29.cloned.1.call-start
  220.1 84.7 %all-reduce.21.cloned.1.call-done = bf16[8192,128]{0,1:T(8,128)(2,1)} async-done(((bf16[8192,128]{0,1:T(8,128)(2,1)}), bf16[8192,128]{0,1:T(8,128)(2,1)}) %all-reduce.21.cloned.1.call-update) | async-done | bytes 2097168 | tf_op jit(solution)/shard_map/psum | solution.py:45
  304.8 17.1 %convolution_convert_fusion.5 = bf16[128,2048]{1,0:T(8,128)(2,1)} fusion(bf16[8192,128]{0,1:T(8,128)(2,1)} %all-reduce.21.cloned.1.call-done, bf16[1,8192,2048]{2,1,0:T(8,128)(2,1)} %param.13), kind=kOutput, calls=%fused_computation.82 | convolution fusion | flops 4305715200 | bytes 36175872 | tf_op jit(solution)/shard_map/dot_general | solution.py:61
  321.9 17.7 %convolution_convert_fusion.6 = bf16[128,2048]{1,0:T(8,128)(2,1)} fusion(bf16[8192,128]{0,1:T(8,128)(2,1)} %all-reduce.17.cloned.1.call-done, bf16[8192,128]{0,1:T(8,128)(2,1)} %all-reduce.21.cloned.1.call-done, bf16[1,2048,8192]{2,1,0:T(8,128)(2,1)} %param.12), kind=kOutput, calls=%fused_computation.83 | convolution fusion | flops 4317249536 | bytes 38273024 | tf_op jit(solution)/shard_map/dot_general | solution.py:66
  339.6 0.0 all-reduce.31.cloned.1.call-start
  339.7 35.2 %all-reduce.29.cloned.1.call-done = (bf16[128,2048]{1,0:T(8,128)(2,1)}, bf16[128,2048]{1,0:T(8,128)(2,1)}) async-done(((bf16[128,2048]{1,0:T(8,128)(2,1)}, bf16[128,2048]{1,0:T(8,128)(2,1)}), (bf16[128,2048]{1,0:T(8,128)(2,1)}, bf16[128,2048]{1,0:T(8,128)(2,1)})) %all-reduce.29.cloned.1.call-update) | async-done | bytes 1048592 | tf_op jit(solution)/shard_map/psum | solution.py:48
  374.9 1.6 fusion.123
  376.5 3.4 collective-permute-start.2
  379.9 10.8 %collective-permute-done.2 = bf16[128,2048]{1,0:T(8,128)(2,1)S(1)} collective-permute-done((bf16[128,2048]{1,0:T(8,128)(2,1)S(1)}, bf16[128,2048]{1,0:T(8,128)(2,1)S(1)}, u32[]{:S(2)}, u32[]{:S(2)}) %collective-permute-start.2) | collective-permute-done | bytes 524320 | tf_op jit(solution)/shard_map/ppermute | solution.py:16
  390.7 0.2 convert_reduce_fusion.1
  391.0 11.7 %all-reduce.2 = (f32[128]{0:T(128)S(1)}, f32[128]{0:T(128)S(1)}, f32[128]{0:T(128)S(1)}, f32[128]{0:T(128)S(1)}) all-reduce(f32[128]{0:T(128)S(1)} %get-tuple-element.69, f32[128]{0:T(128)S(1)} %get-tuple-element.68, f32[128]{0:T(128)S(1)} %get-tuple-element.67, ...), channel_id=1, replica_groups=mesh['section'=2,'row'=4,'tp'=4] {'row'}, use_global_device_ids=true, to_apply=%region_22.23 | all-reduce | flops 512 | bytes 4096 | tf_op jit(solution)/shard_map/psum | solution.py:33
  402.7 1.7 fusion.120
  404.4 1.7 collective-permute-start.1
  406.1 23.0 %convolution_convert_fusion.1 = bf16[8192,128]{0,1:T(8,128)(2,1)} fusion(bf16[1,2,128,2048]{3,2,1,0:T(8,128)(2,1)S(1)} %copy-done, bf16[1,8192,2048]{2,1,0:T(8,128)(2,1)} %param.13), kind=kOutput, calls=%fused_computation.43 | convolution fusion | flops 4296015872 | bytes 36175872 | tf_op jit(solution)/shard_map/dot_general | solution.py:56
  429.1 0.8 copy-done.3
  429.9 16.8 %conditional.4 = (bf16[8192,128]{1,0:T(8,128)(2,1)}) conditional(s32[]{:T(128)} %convert_element_type.151, (bf16[2048,8192]{1,0:T(8,128)(2,1)}, bf16[128,2048]{1,0:T(8,128)(2,1)S(1)}) %tuple.77, (bf16[8192,2048]{1,0:T(8,128)(2,1)}, bf16[128,2048]{1,0:T(8,128)(2,1)S(1)}) %tuple.74), branch_computations={%region_23.24_spmd, %region_24.25_spmd} | conditional | flops 4294967296 | bytes 36175880 | solution.py:129
  430.1 16.6 %fusion.170 = bf16[8192,128]{1,0:T(8,128)(2,1)} fusion(bf16[8192,2048]{1,0:T(8,128)(2,1)} %get-tuple-element.46, bf16[128,2048]{1,0:T(8,128)(2,1)S(1)} %get-tuple-element.47), kind=kOutput, calls=%fused_computation.224 | convolution fusion | flops 4294967296 | bytes 36175872 | tf_op jit(solution)/shard_map/cond/branch_1_fun/dot_general | solution.py:56
  446.7 4.1 copy.6
  450.8 0.3 all-reduce.27.cloned.1.call-start
  451.1 3.9 convert_element_type.154
  455.0 150.3 %all-reduce.31.cloned.1.call-done = (bf16[8192,128]{0,1:T(8,128)(2,1)}, bf16[8192,128]{0,1:T(8,128)(2,1)}) async-done(((bf16[8192,128]{0,1:T(8,128)(2,1)}, bf16[8192,128]{0,1:T(8,128)(2,1)}), (bf16[8192,128]{0,1:T(8,128)(2,1)}, bf16[8192,128]{0,1:T(8,128)(2,1)})) %all-reduce.31.cloned.1.call-update) | async-done | bytes 4194320 | tf_op jit(solution)/shard_map/psum | solution.py:45
  605.3 4.0 convert_element_type.176
  609.3 17.7 %convolution_convert_fusion.4 = bf16[128,2048]{1,0:T(8,128)(2,1)} fusion(bf16[8192,128]{0,1:T(8,128)(2,1)} %get-tuple-element.92, bf16[8192,128]{0,1:T(8,128)(2,1)} %get-tuple-element.93, bf16[1,2048,8192]{2,1,0:T(8,128)(2,1)} %param.12), kind=kOutput, calls=%fused_computation.81 | convolution fusion | flops 4317249536 | bytes 38273024 | tf_op jit(solution)/shard_map/dot_general | solution.py:66
  627.0 29.5 %conditional.5 = (bf16[128,2048]{1,0:T(8,128)(2,1)S(1)}) conditional(s32[]{:T(128)} %convert_element_type.151, (f32[8192,128]{0,1:T(8,128)}, bf16[8192,2048]{1,0:T(8,128)(2,1)}) %tuple.75, (f32[8192,128]{0,1:T(8,128)}, f32[8192,128]{0,1:T(8,128)}, bf16[2048,8192]{1,0:T(8,128)(2,1)}) %tuple.78), branch_computations={%region_26.27_spmd, %region_27.28_spmd} | conditional | flops 4314890240 | bytes 59244552 | solution.py:134
  627.0 5.6 copy.9
  632.6 5.6 copy.8
  638.2 18.3 %fusion.22 = bf16[128,2048]{1,0:T(8,128)(2,1)S(1)} fusion(bf16[2048,8192]{1,0:T(8,128)(2,1)} %get-tuple-element.52, f32[8192,128]{1,0:T(8,128)} %copy.9, f32[8192,128]{1,0:T(8,128)} %copy.8), kind=kOutput, calls=%fused_computation.24 | convolution fusion | flops 4314890240 | bytes 42467328 | tf_op jit(solution)/shard_map/cond/branch_1_fun/dot_general | solution.py:66
  656.5 0.8 copy-done.1
  657.3 0.3 all-reduce.23.cloned.1.call-start
  657.6 34.1 %all-reduce.27.cloned.1.call-done = (bf16[128,2048]{1,0:T(8,128)(2,1)}, bf16[128,2048]{1,0:T(8,128)(2,1)}) async-done(((bf16[128,2048]{1,0:T(8,128)(2,1)}, bf16[128,2048]{1,0:T(8,128)(2,1)}), (bf16[128,2048]{1,0:T(8,128)(2,1)}, bf16[128,2048]{1,0:T(8,128)(2,1)})) %all-reduce.27.cloned.1.call-update) | async-done | bytes 1048592 | tf_op jit(solution)/shard_map/psum | solution.py:48
  691.7 1.9 fusion.79
  693.6 11.7 %all-reduce.1 = (f32[128]{0:T(128)S(1)}, f32[128]{0:T(128)S(1)}) all-reduce(f32[128]{0:T(128)S(1)} %get-tuple-element.72, f32[128]{0:T(128)S(1)} %get-tuple-element.73), channel_id=1, replica_groups=mesh['section'=2,'row'=4,'tp'=4] {'row'}, use_global_device_ids=true, to_apply=%region_38.39 | all-reduce | flops 256 | bytes 2048 | tf_op jit(solution)/shard_map/psum | solution.py:33
  705.3 1.5 fusion.111
  706.9 1.3 collective-permute-start.3
  708.2 11.9 %collective-permute-done.3 = bf16[128,2048]{1,0:T(8,128)(2,1)S(1)} collective-permute-done((bf16[128,2048]{1,0:T(8,128)(2,1)S(1)}, bf16[128,2048]{1,0:T(8,128)(2,1)S(1)}, u32[]{:S(2)}, u32[]{:S(2)}) %collective-permute-start.3) | collective-permute-done | bytes 524320 | tf_op jit(solution)/shard_map/ppermute | solution.py:16
  720.1 16.9 %fusion.34 = bf16[8192,128]{0,1:T(8,128)(2,1)} fusion(bf16[128,2048]{1,0:T(8,128)(2,1)S(1)} %collective-permute-done.3, bf16[1,8192,2048]{2,1,0:T(8,128)(2,1)} %param.13), kind=kOutput, calls=%fused_computation.45 | convolution fusion | flops 4296015872 | bytes 36175872 | tf_op jit(solution)/shard_map/dot_general | solution.py:56
  737.0 0.0 all-reduce.25.cloned.1.call-start
  737.1 83.5 %all-reduce.23.cloned.1.call-done = bf16[8192,128]{0,1:T(8,128)(2,1)} async-done(((bf16[8192,128]{0,1:T(8,128)(2,1)}), bf16[8192,128]{0,1:T(8,128)(2,1)}) %all-reduce.23.cloned.1.call-update) | async-done | bytes 2097168 | tf_op jit(solution)/shard_map/psum | solution.py:45
  820.6 17.7 %convolution_convert_fusion.3 = bf16[128,2048]{1,0:T(8,128)(2,1)} fusion(bf16[8192,128]{0,1:T(8,128)(2,1)} %all-reduce.23.cloned.1.call-done, bf16[8192,128]{0,1:T(8,128)(2,1)} %all-reduce.21.cloned.1.call-done, bf16[1,2048,8192]{2,1,0:T(8,128)(2,1)} %param.12), kind=kOutput, calls=%fused_computation.80 | convolution fusion | flops 4317249536 | bytes 38273024 | tf_op jit(solution)/shard_map/dot_general | solution.py:66
  838.3 32.3 %all-reduce.25.cloned.1.call-done = bf16[128,2048]{1,0:T(8,128)(2,1)} async-done(((bf16[128,2048]{1,0:T(8,128)(2,1)}), bf16[128,2048]{1,0:T(8,128)(2,1)}) %all-reduce.25.cloned.1.call-update) | async-done | bytes 524304 | tf_op jit(solution)/shard_map/psum | solution.py:48
  870.6 1.4 fusion.121
  872.0 11.7 %all-reduce = (f32[128]{0:T(128)S(1)}, f32[128]{0:T(128)S(1)}, f32[128]{0:T(128)S(1)}, f32[128]{0:T(128)S(1)}) all-reduce(f32[128]{0:T(128)S(1)} %get-tuple-element.63, f32[128]{0:T(128)S(1)} %get-tuple-element.62, f32[128]{0:T(128)S(1)} %get-tuple-element.61, ...), channel_id=1, replica_groups=mesh['section'=2,'row'=4,'tp'=4] {'row'}, use_global_device_ids=true, to_apply=%region_44.45 | all-reduce | flops 512 | bytes 4096 | tf_op jit(solution)/shard_map/psum | solution.py:33
  883.7 2.6 fusion.134
  886.3 1.1 maximum_bitcast_fusion
  (32 shorter events, 0.2 us)
Async XLA Ops:
  6.5 120.5 %all-reduce.17.cloned.1.call-start = ((), (), s32[]{:S(2)}) async-start(), calls=%async_computation | async-start | bytes 4194304 | tf_op jit(solution)/shard_map/psum | solution.py:45
  22.4 1.4 copy-start.4
  22.4 1.5 copy-start.6
  42.2 134.3 %copy-start = (bf16[1,2,128,2048]{3,2,1,0:T(8,128)(2,1)S(1)}, bf16[1,2,128,2048]{3,2,1,0:T(8,128)(2,1)}, u32[]{:S(2)}) copy-start(bf16[1,2,128,2048]{3,2,1,0:T(8,128)(2,1)} %param.10) | copy-start | bytes 3145732
  42.2 161.1 %copy-start.2 = (f32[1,2048]{1,0:T(1,128)S(1)}, f32[1,2048]{1,0:T(1,128)}, u32[]{:S(2)}) copy-start(f32[1,2048]{1,0:T(1,128)} %param.11) | copy-start | bytes 24580
  42.2 134.3 %all-reduce.19.cloned.1.call-start = ((), (), s32[]{:S(2)}) async-start(), calls=%async_computation.1 | async-start | bytes 1048576 | tf_op jit(solution)/shard_map/psum | solution.py:48
  144.2 160.6 %all-reduce.21.cloned.1.call-start = ((), (), s32[]{:S(2)}) async-start(), calls=%async_computation.2 | async-start | bytes 4194304 | tf_op jit(solution)/shard_map/psum | solution.py:45
  177.6 13.6 %collective-permute-start = (bf16[128,2048]{1,0:T(8,128)(2,1)S(1)}, bf16[128,2048]{1,0:T(8,128)(2,1)S(1)}, u32[]{:S(2)}, u32[]{:S(2)}) collective-permute-start(bf16[128,2048]{1,0:T(8,128)(2,1)S(1)} %fusion.119), channel_id=1, source_target_pairs={{0,16},{1,17},{2,18},{3,19},{4,20},{5,21},{6,22},{7,23},{8,24},{9,... | collective-permute-start | bytes 1572872 | tf_op jit(solution)/shard_map/ppermute | solution.py:16
  219.8 155.1 %all-reduce.29.cloned.1.call-start = ((), (), s32[]{:S(2)}) async-start(), calls=%async_computation.6 | async-start | bytes 2097152 | tf_op jit(solution)/shard_map/psum | solution.py:48
  339.6 265.7 %all-reduce.31.cloned.1.call-start = ((), (), s32[]{:S(2)}) async-start(), calls=%async_computation.7 | async-start | bytes 8388608 | tf_op jit(solution)/shard_map/psum | solution.py:45
  376.5 14.2 %collective-permute-start.2 = (bf16[128,2048]{1,0:T(8,128)(2,1)S(1)}, bf16[128,2048]{1,0:T(8,128)(2,1)S(1)}, u32[]{:S(2)}, u32[]{:S(2)}) collective-permute-start(bf16[128,2048]{1,0:T(8,128)(2,1)S(1)} %get-tuple-element.97), channel_id=1, source_target_pairs={{0,16},{1,17},{2,18},{3,19},{4,20},{5,21},{6,22},{7,23},{8,24},{9,... | collective-permute-start | bytes 1572872 | tf_op jit(solution)/shard_map/ppermute | solution.py:16
  404.4 24.7 %collective-permute-start.1 = (bf16[128,2048]{1,0:T(8,128)(2,1)S(1)}, bf16[128,2048]{1,0:T(8,128)(2,1)S(1)}, u32[]{:S(2)}, u32[]{:S(2)}) collective-permute-start(bf16[128,2048]{1,0:T(8,128)(2,1)S(1)} %get-tuple-element.98), channel_id=1, source_target_pairs={{16,0},{17,1},{18,2},{19,3},{20,4},{21,5},{22,6},{23,7},{24,8},{25... | collective-permute-start | bytes 1572872 | tf_op jit(solution)/shard_map/ppermute | solution.py:16
  429.1 0.8 copy-start.3
  450.8 240.9 %all-reduce.27.cloned.1.call-start = ((), (), s32[]{:S(2)}) async-start(), calls=%async_computation.5 | async-start | bytes 2097152 | tf_op jit(solution)/shard_map/psum | solution.py:48
  627.0 64.7 %copy-start.5 = (f32[128]{0:T(128)S(1)}, f32[128]{0:T(128)}, u32[]{:S(2)}) copy-start(f32[128]{0:T(128)} %copy-done.4) | copy-start | bytes 1540
  627.0 64.7 %copy-start.7 = (f32[128]{0:T(128)S(1)}, f32[128]{0:T(128)}, u32[]{:S(2)}) copy-start(f32[128]{0:T(128)} %copy-done.6) | copy-start | bytes 1540
  656.5 0.8 copy-start.1
  657.3 163.3 %all-reduce.23.cloned.1.call-start = ((), (), s32[]{:S(2)}) async-start(), calls=%async_computation.3 | async-start | bytes 4194304 | tf_op jit(solution)/shard_map/psum | solution.py:45
  706.9 13.2 %collective-permute-start.3 = (bf16[128,2048]{1,0:T(8,128)(2,1)S(1)}, bf16[128,2048]{1,0:T(8,128)(2,1)S(1)}, u32[]{:S(2)}, u32[]{:S(2)}) collective-permute-start(bf16[128,2048]{1,0:T(8,128)(2,1)S(1)} %fusion.111), channel_id=1, source_target_pairs={{16,0},{17,1},{18,2},{19,3},{20,4},{21,5},{22,6},{23,7},{24,8},{25... | collective-permute-start | bytes 1572872 | tf_op jit(solution)/shard_map/ppermute | solution.py:16
  737.0 133.5 %all-reduce.25.cloned.1.call-start = ((), (), s32[]{:S(2)}) async-start(), calls=%async_computation.4 | async-start | bytes 1048576 | tf_op jit(solution)/shard_map/psum | solution.py:48
Sparse Core Ops, SparseCore 0:
  42.3 84.6 all-reduce.16
  144.3 32.1 all-reduce.18
  219.9 84.7 all-reduce.20
  339.7 35.1 all-reduce.28
  450.9 154.3 all-reduce.30
  657.4 34.2 all-reduce.26
  737.2 83.3 all-reduce.22
  838.4 32.1 all-reduce.24
